TPU v7x, 512 devices: a whole 4x8x8 slice. The times are simulated.
512 devices in a mesh: dp: 2 (over y_lo), storage: 32 (over y_hi, z), feature: 8 (over x, core).
Axes of the slice: x: 4, y: 8 (y_hi: 4, y_lo: 2; y = y_hi * 2 + y_lo), z: 8, core: 2. Of those that a mesh axis runs over, the one named last changes fastest.
Arguments:
- activations: bfloat16 [8192, 4096], P(('dp', 'storage'), 'feature'), may hold values from -6 to 6
- expert_ids: int32 [8192, 1], P(('dp', 'storage')), may hold values from 0 to 1; in each aligned block of 128 rows (0 to 127, 128 to 255, ...) at most 96 rows name the same one
- pre_bias: float32 [2, 4096], P('dp', 'feature'), may hold values from -3 to 3
- enc_weight: bfloat16 [2, 4096, 4096], P('dp', 'feature', 'storage'), may hold values from -0.09375 to 0.09375
- enc_bias: float32 [2, 4096], P('dp'), may hold values from -3 to 3
- dec_weight: bfloat16 [2, 4096, 4096], P('dp', 'feature', 'storage'), may hold values from -0.09375 to 0.09375
Outputs:
- rebuilt: bfloat16 [8192, 4096], P(('dp', 'storage'), 'feature')
- row_error: float32 [8192], P(('dp', 'storage'))
Inputs may be any that keep to these rules, and one draw needn't show every extreme that they name: `expert_ids`: each row names one expert. Among the rows of one index of dp and storage, at most 96 name the same expert, and that bound is reached.
All inputs are finite; a program needn't handle non-finite values.
Results may differ from a plain program's by a relative error of at most 0.018.
Values may be sent and summed in bfloat16 or wider, within the bound.
A program may use at most 64 MiB of HBM per device.

v0:
```python
import jax
import jax.numpy as jnp
from jax import lax
from jax.sharding import PartitionSpec as P

D = 4096
CAP = 96


def local(activations, expert_ids, pre_bias, enc_weight, enc_bias, dec_weight):
    experts = lax.axis_size("dp")
    feat_local = activations.shape[1]
    expert_of = expert_ids[:, 0]
    onehot = (expert_of[:, None] == jnp.arange(experts, dtype=jnp.int32)[None, :]).astype(jnp.int32)
    rank_in = jnp.sum((jnp.cumsum(onehot, 0) - onehot) * onehot, 1)
    slot_of = expert_of * CAP + rank_in
    placer = (slot_of[None, :] == jnp.arange(experts * CAP, dtype=jnp.int32)[:, None]).astype(
        jnp.bfloat16
    )
    outgoing = jnp.dot(placer, activations, preferred_element_type=jnp.float32).astype(jnp.bfloat16)
    incoming = lax.all_to_all(
        outgoing.reshape(experts, CAP, feat_local), "dp", split_axis=0, concat_axis=0, tiled=True
    )
    incoming = incoming.reshape(experts * CAP, feat_local)
    bias_pre = pre_bias[0]
    centred = (incoming.astype(jnp.float32) - bias_pre[None, :]).astype(jnp.bfloat16)
    slot_total = experts * CAP
    columns = jnp.dot(
        centred,
        lax.all_gather(enc_weight, "storage", axis=2, tiled=True)[0],
        preferred_element_type=jnp.float32,
    )
    summed = lax.psum(columns.astype(jnp.bfloat16), "feature").astype(jnp.float32)
    latents = jax.nn.relu(summed + enc_bias[0][None, :]).astype(jnp.bfloat16)
    decoded = lax.dot_general(
        latents,
        lax.all_gather(dec_weight, "storage", axis=2, tiled=True)[0],
        (((1,), (1,)), ((), ())),
        preferred_element_type=jnp.float32,
    )
    rebuilt_slots = (decoded + bias_pre[None, :]).astype(jnp.bfloat16)
    returned = lax.all_to_all(
        rebuilt_slots.reshape(experts, CAP, feat_local),
        "dp",
        split_axis=0,
        concat_axis=0,
        tiled=True,
    )
    returned = returned.reshape(slot_total, feat_local)
    rebuilt = lax.dot_general(
        placer, returned, (((0,), (0,)), ((), ())), preferred_element_type=jnp.float32
    ).astype(jnp.bfloat16)
    diff = rebuilt.astype(jnp.float32) - activations.astype(jnp.float32)
    err_part = jnp.sum(diff * diff, axis=1) / D
    row_error = lax.psum(err_part, "feature")
    return (rebuilt, row_error)


def solution(mesh):
    return jax.shard_map(
        local,
        mesh=mesh,
        in_specs=(
            P(("dp", "storage"), "feature"),
            P(("dp", "storage"), None),
            P("dp", "feature"),
            P("dp", "feature", "storage"),
            P("dp", None),
            P("dp", "feature", "storage"),
        ),
        out_specs=(P(("dp", "storage"), "feature"), P(("dp", "storage"))),
        check_vma=False,
    )
```

profile of v0, /device:TPU:1, one launch (start us, length us, event | category | flops | bytes accessed | tf_op | source)
XLA Modules:
  0.0 326.7 jit_solution(17530223247732946151)
XLA Ops:
  7.2 0.0 all-gather.3.cloned.1.call-start
  7.2 0.7 all-gather.3.cloned.1.call-update
  7.9 0.0 all-gather.5.cloned.1.call-start
  7.9 0.7 all-gather.5.cloned.1.call-update
  8.6 0.0 all-reduce.2.cloned.1.call-start
  8.7 0.7 fusion.11
  9.4 0.2 reduce_window_sum.11
  9.6 0.8 select_reduce_fusion
  10.4 0.7 multiply_add_fusion
  11.1 1.1 convolution_convert_fusion.1
  12.2 6.9 %all_to_all.10 = bf16[2,96,512]{2,1,0:T(8,128)(2,1)S(1)} all-to-all(bf16[2,96,512]{2,1,0:T(8,128)(2,1)S(1)} %bitcast.23), channel_id=1, replica_groups=mesh['dp'=2,'storage'=32,'feature'=8] {'dp'}, dimensions={0} | all-to-all | bytes 393216 | tf_op jit(solution)/shard_map/all_to_all | solution.py:21
  19.1 0.7 subtract_convert_fusion
  19.8 95.8 %all-gather.3.cloned.1.call-done = bf16[1,512,4096]{2,1,0:T(8,128)(2,1)} async-done(((bf16[1,512,128]{2,1,0:T(8,128)(2,1)}), bf16[1,512,4096]{2,1,0:T(8,128)(2,1)}) %all-gather.3.cloned.1.call-update) | async-done | bytes 4194320 | tf_op jit(solution)/shard_map/all_gather | solution.py:30
  115.6 0.0 copy-start.1
  115.6 0.0 copy-start.2
  115.6 4.4 %convolution_convert_fusion = bf16[192,4096]{1,0:T(8,128)(2,1)} fusion(bf16[192,512]{1,0:T(8,128)(2,1)S(1)} %bitcast.21, bf16[1,512,4096]{2,1,0:T(8,128)(2,1)} %all-gather.3.cloned.1.call-done), kind=kOutput, calls=%fused_computation | convolution fusion | flops 806092800 | bytes 5963776 | tf_op jit(solution)/shard_map/dot_general | solution.py:28
  120.1 0.0 all-reduce.2.cloned.1.call-update
  120.1 97.6 %all-gather.5.cloned.1.call-done = bf16[1,512,4096]{2,1,0:T(8,128)(2,1)} async-done(((bf16[1,512,128]{2,1,0:T(8,128)(2,1)}), bf16[1,512,4096]{2,1,0:T(8,128)(2,1)}) %all-gather.5.cloned.1.call-update) | async-done | bytes 4194320 | tf_op jit(solution)/shard_map/all_gather | solution.py:37
  217.7 75.4 %all-reduce.2.cloned.1.call-done = bf16[192,4096]{1,0:T(8,128)(2,1)} async-done(((bf16[192,4096]{1,0:T(8,128)(2,1)}), bf16[192,4096]{1,0:T(8,128)(2,1)}) %all-reduce.2.cloned.1.call-update) | async-done | bytes 1572880 | tf_op jit(solution)/shard_map/psum | solution.py:33
  293.1 0.0 copy-done.1
  293.1 0.0 copy-done.2
  293.1 0.0 copy-start
  293.1 4.2 %fusion.8 = bf16[192,512]{1,0:T(8,128)(2,1)S(1)} fusion(bf16[1,512,4096]{2,1,0:T(8,128)(2,1)} %all-gather.5.cloned.1.call-done, bf16[192,4096]{1,0:T(8,128)(2,1)} %all-reduce.2.cloned.1.call-done, f32[4096]{0:T(1024)S(1)} %bitcast.29, f32[512]{0:T(512)S(1)} %bitcast.26), kind=kOutput, calls=%fused_computation.8 | convolution fusion | flops 808648704 | bytes 5982208 | tf_op jit(solution)/shard_map/dot_general | solution.py:35
  297.3 6.1 %all_to_all.11 = bf16[2,96,512]{2,1,0:T(8,128)(2,1)S(1)} all-to-all(bf16[2,96,512]{2,1,0:T(8,128)(2,1)S(1)} %bitcast.24), channel_id=1, replica_groups=mesh['dp'=2,'storage'=32,'feature'=8] {'dp'}, dimensions={0} | all-to-all | bytes 393216 | tf_op jit(solution)/shard_map/all_to_all | solution.py:42
  303.4 0.0 copy-done
  303.4 0.9 multiply_reduce_fusion
  304.3 15.9 %psum.15 = f32[128]{0:T(128)} all-reduce(f32[128]{0:T(128)S(1)} %broadcast_multiply_fusion), channel_id=1, replica_groups=mesh['dp'=2,'storage'=32,'feature'=8] {'feature'}, use_global_device_ids=true, to_apply=%region_4.5 | all-reduce | flops 128 | bytes 1024 | tf_op jit(solution)/shard_map/psum | solution.py:55
  (1 shorter events, 0.0 us)
Async XLA Ops:
  7.2 108.4 %all-gather.3.cloned.1.call-start = ((), (), s32[]{:S(2)}) async-start(), calls=%async_computation.2 | async-start | bytes 4325376 | tf_op jit(solution)/shard_map/all_gather | solution.py:30
  7.9 209.8 %all-gather.5.cloned.1.call-start = ((), (), s32[]{:S(2)}) async-start(), calls=%async_computation.4 | async-start | bytes 4325376 | tf_op jit(solution)/shard_map/all_gather | solution.py:37
  8.6 284.4 %all-reduce.2.cloned.1.call-start = ((), (), s32[]{:S(2)}) async-start(), calls=%async_computation.3 | async-start | bytes 3145728 | tf_op jit(solution)/shard_map/psum | solution.py:33
  115.6 177.5 %copy-start.1 = (f32[1,512]{1,0:T(1,128)S(1)}, f32[1,512]{1,0:T(1,128)}, u32[]{:S(2)}) copy-start(f32[1,512]{1,0:T(1,128)} %param.8) | copy-start | bytes 6148
  115.6 177.5 %copy-start.2 = (f32[1,4096]{1,0:T(1,128)S(1)}, f32[1,4096]{1,0:T(1,128)}, u32[]{:S(2)}) copy-start(f32[1,4096]{1,0:T(1,128)} %param.10) | copy-start | bytes 49156
  293.1 10.3 %copy-start = (bf16[128,512]{1,0:T(8,128)(2,1)S(1)}, bf16[128,512]{1,0:T(8,128)(2,1)}, u32[]{:S(2)}) copy-start(bf16[128,512]{1,0:T(8,128)(2,1)} %param.6) | copy-start | bytes 393220
Sparse Core Ops, SparseCore 0:
  11.0 104.5 all-gather.2
  118.7 98.9 all-gather.4
  220.0 72.9 all-reduce.1
where the time goes:
time: 327 us
  waiting for transfers between devices  270 us (83%)
  blocking collectives  28.8 us (9%)
  between operations  13.8 us (4%)
  matrix products  10.7 us (3%)
    all_gather x1, waiting for transfers between devices, local(): lax.all_gather(dec_weight, 'storage', axis=2, tiled=True)[0]  97.6 us
    all_gather x1, waiting for transfers between devices, local(): lax.all_gather(enc_weight, 'storage', axis=2, tiled=True)[0]  95.8 us
    psum x1, waiting for transfers between devices, local(): lax.psum(columns.astype(jnp.bfloat16), 'feature').astype(jnp.float32)  75.4 us
    psum x1, blocking collectives, local(): row_error = lax.psum(err_part, 'feature')  15.9 us
    all_to_all x1, blocking collectives, local(): lax.all_to_all(outgoing.reshape(experts, CAP, feat_local), 'dp', split_ax...  6.86 us
  transfers between devices with their start and end apart: 3, of which 3 were waited for; matrix products, arithmetic and copies ran while one was open for 3% of the time, Pallas kernels for 0%

commit v1 on v0

v1 whole, which is shorter than its diff:
```python
import functools

import jax
import jax.numpy as jnp
from jax import lax
from jax.experimental import pallas as pl
from jax.experimental.pallas import tpu as pltpu
from jax.sharding import PartitionSpec as P

MESH = pl.DeviceIdType.MESH
D = 4096
N = 8
NX = 4
ROWS = 128
FEAT = 512
BLK = 128
LATS = 512
CH = 2
F32 = jnp.float32
BF16 = jnp.bfloat16


def ring_steps(direction, chunk):
    far = chunk < CH // 2 if direction == 0 else chunk >= CH // 2
    return 4 if far else 3


def kernel(
    act, ids, pre_bias, enc_w, enc_b, dec_w, out, err,
    a_buf, w_buf, d_buf, meta, ids_all, mask, pair_out, pair_in, x_out, x_in, own_sum, lat, dec, acc_out, acc_in,
    err_all,
    a_ss, a_rs, w_ss, w_rs, d_ss, d_rs, m_ss, m_rs, i_ss, i_rs, p_ss, p_rs, x_ss, x_rs, g_ss, g_rs, s_ss, s_rs,
    o_ss, o_rs, e_ss, e_rs,
):
    dp = lax.axis_index("dp")
    storage = lax.axis_index("storage")
    feature = lax.axis_index("feature")
    z = storage % 8
    y = (storage // 8) * 2 + dp
    x = feature // 2
    c = feature % 2

    def at(yy, zz, ff):
        return (yy % 2, (yy // 2) * 8 + zz, ff)

    def z_at(off):
        return at(y, (z + off + N) % N, feature)

    def y_at(off):
        return at((y + off + N) % N, z, feature)

    def f_at(xx, cc):
        return at(y, z, xx * 2 + cc)

    def w_slot(yy):
        return (yy % 2) * 4 + yy // 2

    pending = []

    def send(src, dst, ss, rs, dev):
        cp = pltpu.make_async_remote_copy(
            src_ref=src, dst_ref=dst, send_sem=ss, recv_sem=rs, device_id=dev, device_id_type=MESH
        )
        cp.start()
        pending.append(cp)

    def arrive(dst, ss, rs):
        pltpu.make_async_remote_copy(
            src_ref=dst, dst_ref=dst, send_sem=ss, recv_sem=rs, device_id=f_at(x, 1 - c), device_id_type=MESH
        ).wait_recv()

    barrier = pltpu.get_barrier_semaphore()
    greet = [z_at(k) for k in range(1, N)] + [y_at(1), y_at(-1)]
    greet += [at(y, z, (feature + k) % 8) for k in range(1, 8)]
    for dev in greet:
        pl.semaphore_signal(barrier, inc=1, device_id=dev, device_id_type=MESH)

    a_buf[z] = act[...]
    w_buf[w_slot(y)] = enc_w[0]
    d_buf[w_slot(y)] = dec_w[0].astype(F32).T.astype(BF16)
    meta[dp, 0:1, :] = pre_bias[...]
    for q in range(4):
        meta[dp, 1:2, q * BLK:(q + 1) * BLK] = enc_b[0:1, pl.ds(pl.multiple_of((q * 8 + z) * BLK, BLK), BLK)]
    ids_all[z] = jnp.broadcast_to(ids[...], (8, ROWS))

    pl.semaphore_wait(barrier, len(greet))

    send(meta.at[dp], meta.at[dp], m_ss, m_rs, at(y + 1 - 2 * dp, z, feature))

    def ring_piece(buf, slot_of, coord, direction, step, chunk):
        sign = 1 if direction == 0 else -1
        block = slot_of((coord - step * sign + N) % N)
        size = buf.shape[1] // CH
        return buf.at[block, pl.ds(chunk * size, size)]

    def ring_send(buf, slot_of, coord, to, ss, rs, direction, step, chunk):
        ref = ring_piece(buf, slot_of, coord, direction, step, chunk)
        sign = 1 if direction == 0 else -1
        send(ref, ref, ss.at[direction, step, chunk], rs.at[direction, step, chunk], to(sign))

    def ring_arrive(buf, slot_of, coord, ss, rs, direction, step, chunk):
        ref = ring_piece(buf, slot_of, coord, direction, step + 1, chunk)
        arrive(ref, ss.at[direction, step, chunk], rs.at[direction, step, chunk])

    a_ring = (a_buf, lambda b: b, z, z_at, a_ss, a_rs)
    w_ring = (w_buf, w_slot, y, y_at, w_ss, w_rs)
    d_ring = (d_buf, w_slot, y, y_at, d_ss, d_rs)

    def gather_step(rings, step):
        for chunk in range(CH):
            for buf, slot_of, coord, to, ss, rs in rings:
                for direction in range(2):
                    steps = ring_steps(direction, chunk)
                    if 1 <= step <= steps:
                        ring_arrive(buf, slot_of, coord, ss, rs, direction, step - 1, chunk)
                    if step < steps:
                        ring_send(buf, slot_of, coord, to, ss, rs, direction, step, chunk)

    gather_step((a_ring, w_ring), 0)
    for k in range(1, N):
        send(ids_all.at[z], ids_all.at[z], i_ss.at[k], i_rs.at[k], z_at(k))

    def mask_of(b):
        mask[b] = jnp.broadcast_to(ids_all[b, 0:1, :].astype(F32), (ROWS, ROWS)).T

    mask_of(z)
    for k in range(1, N):
        src = (z - k + N) % N
        arrive(ids_all.at[src], i_ss.at[k], i_rs.at[k])
        mask_of(src)
    arrive(meta.at[1 - dp], m_ss, m_rs)

    for step in range(1, 5):
        gather_step((a_ring, w_ring), step)

    gather_step((d_ring,), 0)

    def wide(b):
        tile = mask[b]
        return jnp.concatenate([tile] * 4, axis=1) > 0.5

    enc = [jnp.concatenate([w_buf[e * 4 + q] for q in range(4)], axis=1) for e in range(2)]

    def encode(blocks):
        left, right = [], []
        for b in blocks:
            second = wide(b)
            rows = a_buf[b].astype(F32)
            left.append(jnp.where(second, 0.0, rows - meta[0, 0:1, :]).astype(BF16))
            right.append(jnp.where(second, rows - meta[1, 0:1, :], 0.0).astype(BF16))
        return jnp.dot(jnp.concatenate(left, 0), enc[0], preferred_element_type=F32) + jnp.dot(
            jnp.concatenate(right, 0), enc[1], preferred_element_type=F32
        )

    sibling = f_at(x, 1 - c)
    offsets = (2, 1, 3, 0)
    for pair in (offsets[:2], offsets[2:]):
        sums = encode([2 * ((x + o) % NX) + 1 - c for o in pair])
        for j, o in enumerate(pair):
            pair_out[o] = sums[j * ROWS:(j + 1) * ROWS].astype(BF16)
            send(pair_out.at[o], pair_in.at[o], p_ss.at[o], p_rs.at[o], sibling)
    for pair in (offsets[:2], offsets[2:]):
        sums = encode([2 * ((x + o) % NX) + c for o in pair])
        for j, o in enumerate(pair):
            arrive(pair_in.at[o], p_ss.at[o], p_rs.at[o])
            total = sums[j * ROWS:(j + 1) * ROWS] + pair_in[o].astype(F32)
            if o == 0:
                own_sum[...] = total
            else:
                x_out[o] = total.astype(BF16)
                send(x_out.at[o], x_in.at[o], x_ss.at[o], x_rs.at[o], f_at((x + o) % NX, c))

    gather_step((d_ring,), 1)

    for o in range(1, NX):
        arrive(x_in.at[o], x_ss.at[o], x_rs.at[o])
    pre = own_sum[...] + (x_in[1].astype(F32) + x_in[2].astype(F32) + x_in[3].astype(F32))
    pre += jnp.where(wide(feature), meta[1, 1:2, :], meta[0, 1:2, :])
    lat[feature] = jnp.maximum(pre, 0.0).astype(BF16)
    for o in (2, 1, 3):
        send(lat.at[feature], lat.at[feature], g_ss.at[o], g_rs.at[o], f_at((x + o) % NX, c))
    send(lat.at[feature], lat.at[feature], s_ss.at[0], s_rs.at[0], sibling)

    gather_step((d_ring,), 2)
    for o in (1, 3, 2):
        src = 2 * ((x - o + NX) % NX) + c
        arrive(lat.at[src], g_ss.at[o], g_rs.at[o])
        send(lat.at[src], lat.at[src], s_ss.at[o], s_rs.at[o], sibling)
    gather_step((d_ring,), 3)
    gather_step((d_ring,), 4)
    for o in range(NX):
        src = 2 * ((x - o + NX) % NX) + 1 - c
        arrive(lat.at[src], s_ss.at[o], s_rs.at[o])

    weights = d_buf[...].reshape(N * BLK, FEAT)

    def decode(blocks):
        rows = []
        for b in blocks:
            second = wide(b)
            value = lat[b].astype(F32)
            rows.append(
                jnp.concatenate(
                    [jnp.where(second, 0.0, value).astype(BF16), jnp.where(second, value, 0.0).astype(BF16)], axis=1
                )
            )
        return jnp.dot(jnp.concatenate(rows, 0), weights, preferred_element_type=F32)

    half = ROWS // 2

    def hop(direction, step, h, value):
        acc_out[direction, step, h] = value.astype(BF16)
        send(
            acc_out.at[direction, step, h], acc_in.at[direction, step, h],
            o_ss.at[direction, step, h], o_rs.at[direction, step, h], z_at(1 if direction == 0 else -1),
        )

    def landed(direction, step, h):
        arrive(acc_in.at[direction, step, h], o_ss.at[direction, step, h], o_rs.at[direction, step, h])
        return acc_in[direction, step, h].astype(F32)

    part = decode([(z + 4) % N])
    hop(0, 0, 0, part[:half])
    hop(1, 0, 1, part[half:])
    for step in range(1, 4):
        far = 4 - step
        dec[...] = decode([(z + far) % N, (z - far + N) % N])
        for direction in range(2):
            for h in (direction, 1 - direction):
                value = dec[direction * ROWS + h * half:direction * ROWS + (h + 1) * half, :]
                if step > 1 or h == direction:
                    value = value + landed(direction, step - 1, h)
                hop(direction, step, h, value)
    dec[0:ROWS] = decode([z])
    squares = []
    for h in range(2):
        span = slice(h * half, (h + 1) * half)
        total = dec[span, :] + (landed(0, 3, h) + landed(1, 3, h))
        second = jnp.concatenate([mask[z, span, :]] * 4, axis=1) > 0.5
        total += jnp.where(second, meta[1, 0:1, :], meta[0, 0:1, :])
        rebuilt = total.astype(BF16)
        out[span, :] = rebuilt
        diff = rebuilt.astype(F32) - act[span, :].astype(F32)
        square = diff * diff
        squares.append(square[:, 0:128] + square[:, 128:256] + square[:, 256:384] + square[:, 384:512])
    mine = jnp.sum(jnp.concatenate(squares, 0).T, axis=0, keepdims=True)
    err_all[0] = jnp.broadcast_to(mine, (8, ROWS))
    for k in range(1, 8):
        send(err_all.at[0], err_all.at[k], e_ss.at[k], e_rs.at[k], at(y, z, (feature + k) % 8))
    total = mine
    for k in range(1, 8):
        arrive(err_all.at[k], e_ss.at[k], e_rs.at[k])
        total += err_all[k, 0:1, :]
    err[...] = total * (1.0 / D)
    for cp in pending:
        cp.wait_send()


def local(activations, expert_ids, pre_bias, enc_weight, enc_bias, dec_weight):
    vmem = pl.BlockSpec(memory_space=pltpu.VMEM)
    dma = pltpu.SemaphoreType.DMA
    rebuilt, row_error = pl.pallas_call(
        kernel,
        out_shape=(
            jax.ShapeDtypeStruct((ROWS, FEAT), BF16),
            jax.ShapeDtypeStruct((1, ROWS), F32),
        ),
        in_specs=[vmem] * 6,
        out_specs=(vmem, vmem),
        scratch_shapes=[
            pltpu.VMEM((N, ROWS, FEAT), BF16),
            pltpu.VMEM((N, FEAT, BLK), BF16),
            pltpu.VMEM((N, BLK, FEAT), BF16),
            pltpu.VMEM((2, 8, FEAT), F32),
            pltpu.VMEM((N, 8, ROWS), jnp.int32),
            pltpu.VMEM((N, ROWS, ROWS), F32),
            pltpu.VMEM((NX, ROWS, LATS), BF16),
            pltpu.VMEM((NX, ROWS, LATS), BF16),
            pltpu.VMEM((NX, ROWS, LATS), BF16),
            pltpu.VMEM((NX, ROWS, LATS), BF16),
            pltpu.VMEM((ROWS, LATS), F32),
            pltpu.VMEM((N, ROWS, LATS), BF16),
            pltpu.VMEM((2 * ROWS, FEAT), F32),
            pltpu.VMEM((2, 4, 2, ROWS // 2, FEAT), BF16),
            pltpu.VMEM((2, 4, 2, ROWS // 2, FEAT), BF16),
            pltpu.VMEM((N, 8, ROWS), F32),
            dma((2, 4, CH)), dma((2, 4, CH)),
            dma((2, 4, CH)), dma((2, 4, CH)),
            dma((2, 4, CH)), dma((2, 4, CH)),
            dma, dma,
            dma((N,)), dma((N,)),
            dma((NX,)), dma((NX,)),
            dma((NX,)), dma((NX,)),
            dma((NX,)), dma((NX,)),
            dma((NX,)), dma((NX,)),
            dma((2, 4, 2)), dma((2, 4, 2)),
            dma((N,)), dma((N,)),
        ],
        compiler_params=pltpu.CompilerParams(
            collective_id=0, has_side_effects=True, vmem_limit_bytes=48 * 2**20
        ),
    )(activations, expert_ids.reshape(1, ROWS), pre_bias, enc_weight, enc_bias, dec_weight)
    return rebuilt, row_error.reshape(ROWS)


def solution(mesh):
    return jax.shard_map(
        local,
        mesh=mesh,
        in_specs=(
            P(("dp", "storage"), "feature"),
            P(("dp", "storage"), None),
            P("dp", "feature"),
            P("dp", "feature", "storage"),
            P("dp", None),
            P("dp", "feature", "storage"),
        ),
        out_specs=(P(("dp", "storage"), "feature"), P(("dp", "storage"))),
        check_vma=False,
    )
```

time: 327 us -> 87.2 us (0.27)
  waiting for transfers between devices: 270 us -> 0 us
  Pallas kernels: 0 us -> 80.4 us
  blocking collectives: 28.8 us -> 0 us
  between operations: 13.8 us -> 0.65 us
  matrix products: 10.7 us -> 0 us
  local copies, waits for them, and re-layouts: 0.01 us -> 5.93 us
    all_gather x2 -> x0, waiting for transfers between devices: 193 us -> none  [the longest x1 97.6 us: local(): lax.all_gather(dec_weight, 'storage', axis=2, tiled=True)[0]]
    pallas_call x0 -> x1, Pallas kernels: none -> 80.4 us  [local(): pl.pallas_call(kernel, out_shape=(jax.ShapeDtypeStruct((ROWS, FEAT), BF16...]
    psum x1 -> x0, waiting for transfers between devices: 75.4 us -> none  [local(): lax.psum(columns.astype(jnp.bfloat16), 'feature').astype(jnp.float32)]
    psum x1 -> x0, blocking collectives: 15.9 us -> none  [local(): row_error = lax.psum(err_part, 'feature')]
    all_to_all x2 -> x0, blocking collectives: 12.9 us -> none  [the longest x1 6.86 us: local(): lax.all_to_all(outgoing.reshape(experts, CAP, feat_local), 'dp', split_ax...]
    dot_general x4 -> x0, matrix products: 10.7 us -> none  [the longest x1 4.43 us: local(): jnp.dot(centred, lax.all_gather(enc_weight, 'storage', axis=2, tiled=True...]
    unnamed x6 -> x14, local copies, waits for them, and re-layouts: 0.01 us -> 5.93 us
  transfers between devices with their start and end apart: 3 -> 0, of which waited for: 3 -> 0; matrix products, arithmetic and copies ran while one was open for 3% -> 0% of each run, Pallas kernels for 0% -> 0%
where the time goes in v1:
time: 87.2 us; the launch traced here: 87 us
  Pallas kernels  80.4 us (92%)
  local copies, waits for them, and re-layouts  5.93 us (7%)
    pallas_call x1, Pallas kernels, local(): pl.pallas_call(kernel, out_shape=(jax.ShapeDtypeStruct((ROWS, FEAT), BF16...  80.4 us
    unnamed x14, local copies, waits for them, and re-layouts  5.93 us

profile of v1, /device:TPU:1, one launch (start us, length us, event | category | flops | bytes accessed | tf_op | source)
XLA Modules:
  0.0 87.0 jit_solution(5151365355089249362)
XLA Ops:
  0.6 0.0 copy-start.5
  0.6 0.6 copy-done.5
  1.3 0.0 copy-start
  1.3 0.9 %copy-done = bf16[128,512]{1,0:T(8,128)(2,1)S(1)} copy-done((bf16[128,512]{1,0:T(8,128)(2,1)S(1)}, bf16[128,512]{1,0:T(8,128)(2,1)}, u32[]{:S(2)}) %copy-start) | copy-done | bytes 131096
  2.2 0.0 copy-start.1
  2.2 0.9 %copy-done.1 = bf16[1,512,128]{2,1,0:T(8,128)(2,1)S(1)} copy-done((bf16[1,512,128]{2,1,0:T(8,128)(2,1)S(1)}, bf16[1,512,128]{2,1,0:T(8,128)(2,1)}, u32[]{:S(2)}) %copy-start.1) | copy-done | bytes 131096
  3.1 0.0 copy-start.2
  3.1 0.9 %copy-done.2 = bf16[1,512,128]{2,1,0:T(8,128)(2,1)S(1)} copy-done((bf16[1,512,128]{2,1,0:T(8,128)(2,1)S(1)}, bf16[1,512,128]{2,1,0:T(8,128)(2,1)}, u32[]{:S(2)}) %copy-start.2) | copy-done | bytes 131096
  4.0 0.0 copy-start.3
  4.0 0.7 copy-done.3
  4.7 0.0 copy-start.4
  4.7 0.7 copy-done.4
  5.4 80.4 %shard_map.77 = (bf16[128,512]{1,0:T(8,128)(2,1)S(1)}, f32[1,128]{1,0:T(1,128)S(1)}) custom-call(bf16[128,512]{1,0:T(8,128)(2,1)S(1)} %copy-done, s32[1,128]{1,0:T(1,128)S(1)} %bitcast.2, f32[1,512]{1,0:T(1,128)S(1)} %copy-done.4, bf16[1,512,128]{2,1,0:T(8,128)(2,1)S(1)} %copy-done.1, f32[1,4096]{1,0:T(1,128)S(1)} %copy-done.3, ...), custom_call_target="tpu_custom_call" | custom-call | tf_op jit(solution)/shard_map/pallas_call | solution.py:262
  85.8 0.7 copy.10
  86.4 0.5 copy.11
Async XLA Ops:
  0.6 0.7 copy-start.5
  1.3 0.9 %copy-start = (bf16[128,512]{1,0:T(8,128)(2,1)S(1)}, bf16[128,512]{1,0:T(8,128)(2,1)}, u32[]{:S(2)}) copy-start(bf16[128,512]{1,0:T(8,128)(2,1)} %act.1) | copy-start | bytes 393220
  2.2 0.9 %copy-start.1 = (bf16[1,512,128]{2,1,0:T(8,128)(2,1)S(1)}, bf16[1,512,128]{2,1,0:T(8,128)(2,1)}, u32[]{:S(2)}) copy-start(bf16[1,512,128]{2,1,0:T(8,128)(2,1)} %enc_w.1) | copy-start | bytes 393220
  3.1 0.9 %copy-start.2 = (bf16[1,512,128]{2,1,0:T(8,128)(2,1)S(1)}, bf16[1,512,128]{2,1,0:T(8,128)(2,1)}, u32[]{:S(2)}) copy-start(bf16[1,512,128]{2,1,0:T(8,128)(2,1)} %dec_w.1) | copy-start | bytes 393220
  4.0 0.7 copy-start.3
  4.7 0.7 copy-start.4

commit v2 on v1

v2 whole, which is shorter than its diff:
```python
import functools

import jax
import jax.numpy as jnp
from jax import lax
from jax.experimental import pallas as pl
from jax.experimental.pallas import tpu as pltpu
from jax.sharding import PartitionSpec as P

MESH = pl.DeviceIdType.MESH
D = 4096
N = 8
NX = 4
ROWS = 128
FEAT = 512
BLK = 128
LATS = 512
GATHER = 4
DCH = 2
K = 4
SUB = ROWS // K
F32 = jnp.float32
BF16 = jnp.bfloat16


def ring_steps(direction, chunk, chunks):
    far = chunk < chunks // 2 if direction == 0 else chunk >= chunks // 2
    return 4 if far else 3


def kernel(
    act, ids, pre_bias, enc_w, enc_b, dec_w, out, err,
    a_buf, w_buf, w_cat, d_raw, d_buf, pb_raw, eb_raw, ids_raw, meta, ids_all, mask,
    pair_own, pair_out, pair_in, x_own, x_out, x_in, lat, dec, acc_out, acc_in, square, err_all,
    l_sem, a_ss, a_rs, w_ss, w_rs, d_ss, d_rs, m_ss, m_rs, i_ss, i_rs, p_ss, p_rs, x_ss, x_rs, g_ss, g_rs, s_ss, s_rs,
    o_ss, o_rs, e_ss, e_rs,
):
    dp = lax.axis_index("dp")
    storage = lax.axis_index("storage")
    feature = lax.axis_index("feature")
    z = storage % 8
    y = (storage // 8) * 2 + dp
    x = feature // 2
    c = feature % 2

    def at(yy, zz, ff):
        return (yy % 2, (yy // 2) * 8 + zz, ff)

    def z_at(off):
        return at(y, (z + off + N) % N, feature)

    def y_at(off):
        return at((y + off + N) % N, z, feature)

    def f_at(xx, cc):
        return at(y, z, xx * 2 + cc)

    def w_slot(yy):
        return (yy % 2) * 4 + yy // 2

    sibling = f_at(x, 1 - c)
    pending = []

    def send(src, dst, ss, rs, dev):
        cp = pltpu.make_async_remote_copy(
            src_ref=src, dst_ref=dst, send_sem=ss, recv_sem=rs, device_id=dev, device_id_type=MESH
        )
        cp.start()
        pending.append(cp)

    def arrive(dst, ss, rs):
        pltpu.make_async_remote_copy(
            src_ref=dst, dst_ref=dst, send_sem=ss, recv_sem=rs, device_id=sibling, device_id_type=MESH
        ).wait_recv()

    barrier = pltpu.get_barrier_semaphore()
    greet = [z_at(k) for k in range(1, N)] + [y_at(1), y_at(-1)]
    greet += [at(y, z, (feature + k) % 8) for k in range(1, 8)]
    for dev in greet:
        pl.semaphore_signal(barrier, inc=1, device_id=dev, device_id_type=MESH)

    loads = [
        pltpu.make_async_copy(src, dst, l_sem.at[j])
        for j, (src, dst) in enumerate(
            (
                (dec_w.at[0], d_raw),
                (act, a_buf.at[z]),
                (enc_w.at[0], w_buf.at[w_slot(y)]),
                (ids, ids_raw),
                (pre_bias, pb_raw),
                (enc_b, eb_raw),
            )
        )
    ]
    for cp in loads:
        cp.start()
    for cp in loads:
        cp.wait()
    d_buf[w_slot(y)] = d_raw[...].astype(F32).T.astype(BF16)
    meta[dp, 0:1, :] = pb_raw[...]
    for q in range(4):
        meta[dp, 1:2, q * BLK:(q + 1) * BLK] = eb_raw[0:1, pl.ds(pl.multiple_of((q * 8 + z) * BLK, BLK), BLK)]
    ids_all[z] = jnp.broadcast_to(ids_raw[...], (8, ROWS))

    pl.semaphore_wait(barrier, len(greet))

    def ring_piece(buf, slot_of, coord, chunks, direction, step, chunk):
        sign = 1 if direction == 0 else -1
        block = slot_of((coord - step * sign + N) % N)
        size = buf.shape[1] // chunks
        return buf.at[block, pl.ds(chunk * size, size)]

    def ring_send(buf, slot_of, coord, chunks, to, ss, rs, direction, step, chunk):
        ref = ring_piece(buf, slot_of, coord, chunks, direction, step, chunk)
        sign = 1 if direction == 0 else -1
        send(ref, ref, ss.at[direction, step, chunk], rs.at[direction, step, chunk], to(sign))

    def ring_arrive(buf, slot_of, coord, chunks, ss, rs, direction, step, chunk):
        ref = ring_piece(buf, slot_of, coord, chunks, direction, step + 1, chunk)
        arrive(ref, ss.at[direction, step, chunk], rs.at[direction, step, chunk])

    a_ring = (a_buf, lambda b: b, z, GATHER, z_at, a_ss, a_rs)
    w_ring = (w_buf, w_slot, y, GATHER, y_at, w_ss, w_rs)
    d_ring = (d_buf, w_slot, y, DCH, y_at, d_ss, d_rs)

    def gather_step(rings, step):
        for chunk in range(rings[0][3]):
            for buf, slot_of, coord, chunks, to, ss, rs in rings:
                for direction in range(2):
                    steps = ring_steps(direction, chunk, chunks)
                    if 1 <= step <= steps:
                        ring_arrive(buf, slot_of, coord, chunks, ss, rs, direction, step - 1, chunk)
                    if step < steps:
                        ring_send(buf, slot_of, coord, chunks, to, ss, rs, direction, step, chunk)

    def spread(yy):
        lanes = pl.ds(pl.multiple_of((yy // 2) * BLK, BLK), BLK)
        w_cat[yy % 2, :, lanes] = w_buf[w_slot(yy)]

    gather_step((a_ring, w_ring), 0)
    send(meta.at[dp], meta.at[dp], m_ss, m_rs, at(y + 1 - 2 * dp, z, feature))
    for k in range(1, N):
        send(ids_all.at[z], ids_all.at[z], i_ss.at[k], i_rs.at[k], z_at(k))

    def mask_of(b):
        mask[b] = jnp.broadcast_to(ids_all[b, 0:1, :].astype(F32), (ROWS, ROWS)).T

    mask_of(z)
    spread(y)
    gather_step((a_ring, w_ring), 1)
    for k in range(1, N):
        src = (z - k + N) % N
        arrive(ids_all.at[src], i_ss.at[k], i_rs.at[k])
        mask_of(src)
    arrive(meta.at[1 - dp], m_ss, m_rs)
    for step in range(2, 5):
        spread((y + step - 1) % N)
        spread((y - step + 1 + N) % N)
        gather_step((a_ring, w_ring), step)
        if step == 3:
            gather_step((d_ring,), 0)
    spread((y + 4) % N)

    def wide(b, k):
        return jnp.concatenate([mask[b, k * SUB:(k + 1) * SUB, :]] * 4, axis=1) > 0.5

    offsets = (2, 1, 3, 0)

    def encode(k):
        left, right = [], []
        for b in [2 * ((x + o) % NX) + 1 - c for o in offsets] + [2 * ((x + o) % NX) + c for o in offsets]:
            second = wide(b, k)
            rows = a_buf[b, k * SUB:(k + 1) * SUB, :].astype(F32)
            left.append(jnp.where(second, 0.0, rows - meta[0, 0:1, :]).astype(BF16))
            right.append(jnp.where(second, rows - meta[1, 0:1, :], 0.0).astype(BF16))
        sums = jnp.dot(jnp.concatenate(left, 0), w_cat[0], preferred_element_type=F32) + jnp.dot(
            jnp.concatenate(right, 0), w_cat[1], preferred_element_type=F32
        )
        pair_out[k] = sums[:NX * SUB].astype(BF16)
        send(pair_out.at[k], pair_in.at[k], p_ss.at[k], p_rs.at[k], sibling)
        pair_own[k] = sums[NX * SUB:]

    def pair_sum(k):
        arrive(pair_in.at[k], p_ss.at[k], p_rs.at[k])
        total = pair_own[k] + pair_in[k].astype(F32)
        x_own[k] = total[3 * SUB:]
        x_out[k] = total[:3 * SUB].astype(BF16).reshape(3, SUB, LATS)
        for j in range(3):
            send(x_out.at[k, j], x_in.at[k, j], x_ss.at[k, j], x_rs.at[k, j], f_at((x + offsets[j]) % NX, c))

    def activate(k):
        for j in range(3):
            arrive(x_in.at[k, j], x_ss.at[k, j], x_rs.at[k, j])
        pre = x_own[k] + (x_in[k, 0].astype(F32) + x_in[k, 1].astype(F32) + x_in[k, 2].astype(F32))
        pre += jnp.where(wide(feature, k), meta[1, 1:2, :], meta[0, 1:2, :])
        lat[k, c, x] = jnp.maximum(pre, 0.0).astype(BF16)
        mine = lat.at[k, c, x]
        for j in range(3):
            send(mine, mine, g_ss.at[k, j], g_rs.at[k, j], f_at((x + offsets[j]) % NX, c))

    def share(k):
        for j in (1, 2, 0):
            got = lat.at[k, c, (x - offsets[j] + NX) % NX]
            arrive(got, g_ss.at[k, j], g_rs.at[k, j])
        send(lat.at[k, c], lat.at[k, c], s_ss.at[k], s_rs.at[k], sibling)

    def z_far(direction, k):
        return 4 if k % 2 == direction else 3

    def hop(direction, step, k, value):
        acc_out[direction, step, k] = value.astype(BF16)
        send(
            acc_out.at[direction, step, k], acc_in.at[direction, step, k],
            o_ss.at[direction, step, k], o_rs.at[direction, step, k], z_at(1 if direction == 0 else -1),
        )

    def landed(direction, step, k):
        arrive(acc_in.at[direction, step, k], o_ss.at[direction, step, k], o_rs.at[direction, step, k])
        return acc_in[direction, step, k].astype(F32)

    targets = (4, 3, -3, 2, -2, 1, -1, 0)

    def decode(k):
        arrive(lat.at[k, 1 - c], s_ss.at[k], s_rs.at[k])
        rows = []
        for t in targets:
            b = (z + t + N) % N
            second = wide(b, k)
            value = lat[k, b % 2, b // 2].astype(F32)
            rows.append(
                jnp.concatenate(
                    [jnp.where(second, 0.0, value).astype(BF16), jnp.where(second, value, 0.0).astype(BF16)], axis=1
                )
            )
        dec[k] = jnp.dot(
            jnp.concatenate(rows, 0), d_buf[...].reshape(N * BLK, FEAT), preferred_element_type=F32
        ).reshape(N, SUB, FEAT)
        hop(k % 2, 0, k, dec[k, 0])

    def z_step(k, step):
        for direction in (k % 2, 1 - k % 2):
            value = dec[k, 2 * step - 1 + direction]
            if step > 1 or z_far(direction, k) == 4:
                value = value + landed(direction, step - 1, k)
            hop(direction, step, k, value)

    def finish(k):
        span = slice(k * SUB, (k + 1) * SUB)
        total = dec[k, 7] + (landed(k % 2, 3, k) + landed(1 - k % 2, 3, k))
        total += jnp.where(wide(z, k), meta[1, 0:1, :], meta[0, 0:1, :])
        rebuilt = total.astype(BF16)
        out[span, :] = rebuilt
        diff = rebuilt.astype(F32) - a_buf[z, span, :].astype(F32)
        sq = diff * diff
        square[span, :] = sq[:, 0:128] + sq[:, 128:256] + sq[:, 256:384] + sq[:, 384:512]

    encode(0)
    encode(1)
    pair_sum(0)
    encode(2)
    pair_sum(1)
    encode(3)
    pair_sum(2)
    pair_sum(3)
    gather_step((d_ring,), 1)
    activate(0)
    gather_step((d_ring,), 2)
    activate(1)
    activate(2)
    gather_step((d_ring,), 3)
    activate(3)
    share(0)
    gather_step((d_ring,), 4)
    share(1)
    decode(0)
    share(2)
    decode(1)
    z_step(0, 1)
    share(3)
    decode(2)
    z_step(1, 1)
    decode(3)
    z_step(0, 2)
    z_step(2, 1)
    z_step(1, 2)
    z_step(3, 1)
    z_step(0, 3)
    z_step(2, 2)
    z_step(1, 3)
    z_step(3, 2)
    finish(0)
    z_step(2, 3)
    finish(1)
    z_step(3, 3)
    finish(2)
    finish(3)

    mine = jnp.sum(square[...].T, axis=0, keepdims=True)
    err_all[0] = jnp.broadcast_to(mine, (8, ROWS))
    for k in range(1, 8):
        send(err_all.at[0], err_all.at[k], e_ss.at[k], e_rs.at[k], at(y, z, (feature + k) % 8))
    total = mine
    for k in range(1, 8):
        arrive(err_all.at[k], e_ss.at[k], e_rs.at[k])
        total += err_all[k, 0:1, :]
    err[...] = total * (1.0 / D)
    for cp in pending:
        cp.wait_send()


def local(activations, expert_ids, pre_bias, enc_weight, enc_bias, dec_weight):
    vmem = pl.BlockSpec(memory_space=pltpu.VMEM)
    dma = pltpu.SemaphoreType.DMA
    rebuilt, row_error = pl.pallas_call(
        kernel,
        out_shape=(
            jax.ShapeDtypeStruct((ROWS, FEAT), BF16),
            jax.ShapeDtypeStruct((1, ROWS), F32),
        ),
        in_specs=[pl.BlockSpec(memory_space=pltpu.HBM)] * 6,
        out_specs=(vmem, vmem),
        scratch_shapes=[
            pltpu.VMEM((N, ROWS, FEAT), BF16),
            pltpu.VMEM((N, FEAT, BLK), BF16),
            pltpu.VMEM((2, FEAT, LATS), BF16),
            pltpu.VMEM((FEAT, BLK), BF16),
            pltpu.VMEM((N, BLK, FEAT), BF16),
            pltpu.VMEM((1, FEAT), F32),
            pltpu.VMEM((1, D), F32),
            pltpu.VMEM((1, ROWS), jnp.int32),
            pltpu.VMEM((2, 8, FEAT), F32),
            pltpu.VMEM((N, 8, ROWS), jnp.int32),
            pltpu.VMEM((N, ROWS, ROWS), F32),
            pltpu.VMEM((K, NX * SUB, LATS), F32),
            pltpu.VMEM((K, NX * SUB, LATS), BF16),
            pltpu.VMEM((K, NX * SUB, LATS), BF16),
            pltpu.VMEM((K, SUB, LATS), F32),
            pltpu.VMEM((K, 3, SUB, LATS), BF16),
            pltpu.VMEM((K, 3, SUB, LATS), BF16),
            pltpu.VMEM((K, 2, NX, SUB, LATS), BF16),
            pltpu.VMEM((K, N, SUB, FEAT), F32),
            pltpu.VMEM((2, 4, K, SUB, FEAT), BF16),
            pltpu.VMEM((2, 4, K, SUB, FEAT), BF16),
            pltpu.VMEM((ROWS, 128), F32),
            pltpu.VMEM((N, 8, ROWS), F32),
            dma((6,)),
            dma((2, 4, GATHER)), dma((2, 4, GATHER)),
            dma((2, 4, GATHER)), dma((2, 4, GATHER)),
            dma((2, 4, DCH)), dma((2, 4, DCH)),
            dma, dma,
            dma((N,)), dma((N,)),
            dma((K,)), dma((K,)),
            dma((K, 3)), dma((K, 3)),
            dma((K, 3)), dma((K, 3)),
            dma((K,)), dma((K,)),
            dma((2, 4, K)), dma((2, 4, K)),
            dma((N,)), dma((N,)),
        ],
        compiler_params=pltpu.CompilerParams(
            collective_id=0, has_side_effects=True, vmem_limit_bytes=64 * 2**20
        ),
    )(activations, expert_ids.reshape(1, ROWS), pre_bias, enc_weight, enc_bias, dec_weight)
    return rebuilt, row_error.reshape(ROWS)


def solution(mesh):
    return jax.shard_map(
        local,
        mesh=mesh,
        in_specs=(
            P(("dp", "storage"), "feature"),
            P(("dp", "storage"), None),
            P("dp", "feature"),
            P("dp", "feature", "storage"),
            P("dp", None),
            P("dp", "feature", "storage"),
        ),
        out_specs=(P(("dp", "storage"), "feature"), P(("dp", "storage"))),
        check_vma=False,
    )
```

time: 87.2 us -> 77.3 us (0.89)
  Pallas kernels: 80.4 us -> 74.4 us
  local copies, waits for them, and re-layouts: 5.93 us -> 2.08 us
    pallas_call x1, Pallas kernels: 80.4 us -> 74.4 us  [local(): pl.pallas_call(kernel, out_shape=(jax.ShapeDtypeStruct((ROWS, FEAT), BF16...]
    unnamed x14 -> x4, local copies, waits for them, and re-layouts: 5.93 us -> 2.08 us
where the time goes in v2:
time: 77.3 us; the launch traced here: 77.1 us
  Pallas kernels  74.4 us (96%)
  local copies, waits for them, and re-layouts  2.08 us (3%)
    pallas_call x1, Pallas kernels, local(): pl.pallas_call(kernel, out_shape=(jax.ShapeDtypeStruct((ROWS, FEAT), BF16...  74.4 us
    unnamed x4, local copies, waits for them, and re-layouts  2.08 us

profile of v2, /device:TPU:1, one launch (start us, length us, event | category | flops | bytes accessed | tf_op | source)
XLA Modules:
  0.0 77.1 jit_solution(1521856739030838338)
XLA Ops:
  0.6 74.4 %shard_map.77 = (bf16[128,512]{1,0:T(8,128)(2,1)}, f32[1,128]{1,0:T(1,128)}) custom-call(bf16[128,512]{1,0:T(8,128)(2,1)} %act.1, s32[1,128]{1,0:T(1,128)} %bitcast.2, f32[1,512]{1,0:T(1,128)} %pre_bias.1, bf16[1,512,128]{2,1,0:T(8,128)(2,1)} %enc_w.1, f32[1,4096]{1,0:T(1,128)} %enc_b.1, bf16[1,512,128]{2,1,0:T(8,128)(2,1)} %dec_w.1), custom_call_target="tpu_custom_call" | custom-call | tf_op jit(solution)/shard_map/pallas_call | solution.py:314
  75.0 0.0 copy-start
  75.1 1.6 %copy.10 = bf16[128,512]{1,0:T(8,128)(2,1)} copy(bf16[128,512]{1,0:T(8,128)(2,1)} %get-tuple-element.8) | data formatting | bytes 262144
  76.6 0.0 copy-done
  76.6 0.5 copy.11
Async XLA Ops:
  75.0 1.6 %copy-start = (f32[1,128]{1,0:T(1,128)S(1)}, f32[1,128]{1,0:T(1,128)}, u32[]{:S(2)}) copy-start(f32[1,128]{1,0:T(1,128)} %get-tuple-element.5) | copy-start | bytes 1540

commit v3 on v2

--- a/solution.py
+++ b/solution.py
@@ -16,9 +16,12 @@
 BLK = 128
 LATS = 512
 GATHER = 4
-DCH = 2
-K = 4
-SUB = ROWS // K
+PARTS = ((4,), (3, -3), (2, -2), (1, -1, 0))
+K = len(PARTS)
+STRIPE = 16
+MOST = STRIPE * max(len(p) for p in PARTS)
+ZCH = 4
+CHUNK = ROWS // ZCH
 F32 = jnp.float32
 BF16 = jnp.bfloat16
 
@@ -121,10 +124,8 @@
 
     a_ring = (a_buf, lambda b: b, z, GATHER, z_at, a_ss, a_rs)
     w_ring = (w_buf, w_slot, y, GATHER, y_at, w_ss, w_rs)
-    d_ring = (d_buf, w_slot, y, DCH, y_at, d_ss, d_rs)
-
     def gather_step(rings, step):
-        for chunk in range(rings[0][3]):
+        for chunk in range(GATHER):
             for buf, slot_of, coord, chunks, to, ss, rs in rings:
                 for direction in range(2):
                     steps = ring_steps(direction, chunk, chunks)
@@ -137,10 +138,30 @@
         lanes = pl.ds(pl.multiple_of((yy // 2) * BLK, BLK), BLK)
         w_cat[yy % 2, :, lanes] = w_buf[w_slot(yy)]
 
+    def d_piece(direction, hop, piece):
+        size = BLK // 4 if hop == 0 else BLK // 2
+        block = w_slot((y - hop * (1 - 2 * direction) + N) % N)
+        return d_buf.at[block, pl.ds(piece * size, size)], d_ss.at[direction, hop, piece], d_rs.at[direction, hop, piece]
+
+    def d_send(hop, piece):
+        for direction in range(2):
+            if hop < 3 or piece == direction:
+                ref, ss, rs = d_piece(direction, hop, piece)
+                send(ref, ref, ss, rs, y_at(1 - 2 * direction))
+
+    def d_arrive(hop, piece):
+        for direction in range(2):
+            if hop < 3 or piece == direction:
+                ref, ss, rs = d_piece(direction, hop, piece)
+                size = ref.shape[0]
+                block = w_slot((y - (hop + 1) * (1 - 2 * direction) + N) % N)
+                arrive(d_buf.at[block, pl.ds(piece * size, size)], ss, rs)
+
     gather_step((a_ring, w_ring), 0)
     send(meta.at[dp], meta.at[dp], m_ss, m_rs, at(y + 1 - 2 * dp, z, feature))
     for k in range(1, N):
         send(ids_all.at[z], ids_all.at[z], i_ss.at[k], i_rs.at[k], z_at(k))
+    d_send(0, 0)
 
     def mask_of(b):
         mask[b] = jnp.broadcast_to(ids_all[b, 0:1, :].astype(F32), (ROWS, ROWS)).T
@@ -148,152 +169,193 @@
     mask_of(z)
     spread(y)
     gather_step((a_ring, w_ring), 1)
+    d_send(0, 1)
     for k in range(1, N):
         src = (z - k + N) % N
         arrive(ids_all.at[src], i_ss.at[k], i_rs.at[k])
         mask_of(src)
     arrive(meta.at[1 - dp], m_ss, m_rs)
-    for step in range(2, 5):
-        spread((y + step - 1) % N)
-        spread((y - step + 1 + N) % N)
-        gather_step((a_ring, w_ring), step)
-        if step == 3:
-            gather_step((d_ring,), 0)
+    gather_step((a_ring, w_ring), 2)
+    d_send(0, 2)
+    d_send(0, 3)
+    spread((y + 1) % N)
+    spread((y + 7) % N)
+    gather_step((a_ring, w_ring), 3)
+    spread((y + 2) % N)
+    spread((y + 6) % N)
+    for piece in range(4):
+        d_arrive(0, piece)
+    d_send(1, 0)
+    d_send(1, 1)
+    spread((y + 3) % N)
+    spread((y + 5) % N)
+    gather_step((a_ring, w_ring), 4)
     spread((y + 4) % N)
 
-    def wide(b, k):
-        return jnp.concatenate([mask[b, k * SUB:(k + 1) * SUB, :]] * 4, axis=1) > 0.5
+    def wide(tile):
+        return jnp.concatenate([tile] * 4, axis=1) > 0.5
+
+    def stripe(f):
+        return pl.ds(pl.multiple_of(f * STRIPE, STRIPE), STRIPE)
 
     offsets = (2, 1, 3, 0)
+
+    def blocks_of(k):
+        return [(z + t + N) % N for t in PARTS[k]]
 
     def encode(k):
         left, right = [], []
-        for b in [2 * ((x + o) % NX) + 1 - c for o in offsets] + [2 * ((x + o) % NX) + c for o in offsets]:
-            second = wide(b, k)
-            rows = a_buf[b, k * SUB:(k + 1) * SUB, :].astype(F32)
-            left.append(jnp.where(second, 0.0, rows - meta[0, 0:1, :]).astype(BF16))
-            right.append(jnp.where(second, rows - meta[1, 0:1, :], 0.0).astype(BF16))
+        for f in [2 * ((x + o) % NX) + 1 - c for o in offsets] + [2 * ((x + o) % NX) + c for o in offsets]:
+            for b in blocks_of(k):
+                second = wide(mask[b, stripe(f), :])
+                rows = a_buf[b, stripe(f), :].astype(F32)
+                left.append(jnp.where(second, 0.0, rows - meta[0, 0:1, :]).astype(BF16))
+                right.append(jnp.where(second, rows - meta[1, 0:1, :], 0.0).astype(BF16))
         sums = jnp.dot(jnp.concatenate(left, 0), w_cat[0], preferred_element_type=F32) + jnp.dot(
             jnp.concatenate(right, 0), w_cat[1], preferred_element_type=F32
         )
-        pair_out[k] = sums[:NX * SUB].astype(BF16)
-        send(pair_out.at[k], pair_in.at[k], p_ss.at[k], p_rs.at[k], sibling)
-        pair_own[k] = sums[NX * SUB:]
+        half = NX * STRIPE * len(PARTS[k])
+        pair_out[k, :half] = sums[:half].astype(BF16)
+        send(pair_out.at[k, pl.ds(0, half)], pair_in.at[k, pl.ds(0, half)], p_ss.at[k], p_rs.at[k], sibling)
+        pair_own[k, :half] = sums[half:]
 
     def pair_sum(k):
-        arrive(pair_in.at[k], p_ss.at[k], p_rs.at[k])
-        total = pair_own[k] + pair_in[k].astype(F32)
-        x_own[k] = total[3 * SUB:]
-        x_out[k] = total[:3 * SUB].astype(BF16).reshape(3, SUB, LATS)
+        each = STRIPE * len(PARTS[k])
+        got = pair_in.at[k, pl.ds(0, NX * each)]
+        arrive(got, p_ss.at[k], p_rs.at[k])
+        total = pair_own[k, :NX * each] + got[...].astype(F32)
+        x_own[k, :each] = total[3 * each:]
         for j in range(3):
-            send(x_out.at[k, j], x_in.at[k, j], x_ss.at[k, j], x_rs.at[k, j], f_at((x + offsets[j]) % NX, c))
+            x_out[k, j, :each] = total[j * each:(j + 1) * each].astype(BF16)
+            send(
+                x_out.at[k, j, pl.ds(0, each)], x_in.at[k, j, pl.ds(0, each)], x_ss.at[k, j], x_rs.at[k, j],
+                f_at((x + offsets[j]) % NX, c),
+            )
+
+    def lat_of(k, xx):
+        each = STRIPE * len(PARTS[k])
+        return lat.at[k, c, pl.ds(pl.multiple_of(xx * each, STRIPE), each)]
 
     def activate(k):
+        each = STRIPE * len(PARTS[k])
+        pre = x_own[k, :each]
         for j in range(3):
-            arrive(x_in.at[k, j], x_ss.at[k, j], x_rs.at[k, j])
-        pre = x_own[k] + (x_in[k, 0].astype(F32) + x_in[k, 1].astype(F32) + x_in[k, 2].astype(F32))
-        pre += jnp.where(wide(feature, k), meta[1, 1:2, :], meta[0, 1:2, :])
-        lat[k, c, x] = jnp.maximum(pre, 0.0).astype(BF16)
-        mine = lat.at[k, c, x]
+            arrive(x_in.at[k, j, pl.ds(0, each)], x_ss.at[k, j], x_rs.at[k, j])
+            pre = pre + x_in[k, j, :each].astype(F32)
+        second = jnp.concatenate([wide(mask[b, stripe(feature), :]) for b in blocks_of(k)], 0)
+        pre += jnp.where(second, meta[1, 1:2, :], meta[0, 1:2, :])
+        mine = lat_of(k, x)
+        mine[...] = jnp.maximum(pre, 0.0).astype(BF16)
         for j in range(3):
             send(mine, mine, g_ss.at[k, j], g_rs.at[k, j], f_at((x + offsets[j]) % NX, c))
 
     def share(k):
         for j in (1, 2, 0):
-            got = lat.at[k, c, (x - offsets[j] + NX) % NX]
-            arrive(got, g_ss.at[k, j], g_rs.at[k, j])
-        send(lat.at[k, c], lat.at[k, c], s_ss.at[k], s_rs.at[k], sibling)
-
-    def z_far(direction, k):
-        return 4 if k % 2 == direction else 3
-
-    def hop(direction, step, k, value):
-        acc_out[direction, step, k] = value.astype(BF16)
+            arrive(lat_of(k, (x - offsets[j] + NX) % NX), g_ss.at[k, j], g_rs.at[k, j])
+        whole = lat.at[k, c, pl.ds(0, NX * STRIPE * len(PARTS[k]))]
+        send(whole, whole, s_ss.at[k], s_rs.at[k], sibling)
+
+    def decode(k):
+        each = STRIPE * len(PARTS[k])
+        arrive(lat.at[k, 1 - c, pl.ds(0, NX * each)], s_ss.at[k], s_rs.at[k])
+        left, right = [], []
+        for i, b in enumerate(blocks_of(k)):
+            second = wide(mask[b])
+            starts = [(f % 2, (f // 2) * each + i * STRIPE) for f in range(8)]
+            value = jnp.concatenate([lat[k, core, start:start + STRIPE, :] for core, start in starts], 0).astype(F32)
+            left.append(jnp.where(second, 0.0, value).astype(BF16))
+            right.append(jnp.where(second, value, 0.0).astype(BF16))
+        rows = jnp.concatenate([jnp.concatenate(left, 0), jnp.concatenate(right, 0)], axis=1)
+        sums = jnp.dot(rows, d_buf[...].reshape(N * BLK, FEAT), preferred_element_type=F32)
+        first = sum(len(p) for p in PARTS[:k])
+        for i in range(len(PARTS[k])):
+            dec[first + i] = sums[i * ROWS:(i + 1) * ROWS]
+
+    def hop(direction, step, h, value):
+        acc_out[direction, step, h] = value.astype(BF16)
         send(
-            acc_out.at[direction, step, k], acc_in.at[direction, step, k],
-            o_ss.at[direction, step, k], o_rs.at[direction, step, k], z_at(1 if direction == 0 else -1),
+            acc_out.at[direction, step, h], acc_in.at[direction, step, h],
+            o_ss.at[direction, step, h], o_rs.at[direction, step, h], z_at(1 - 2 * direction),
         )
 
-    def landed(direction, step, k):
-        arrive(acc_in.at[direction, step, k], o_ss.at[direction, step, k], o_rs.at[direction, step, k])
-        return acc_in[direction, step, k].astype(F32)
-
-    targets = (4, 3, -3, 2, -2, 1, -1, 0)
-
-    def decode(k):
-        arrive(lat.at[k, 1 - c], s_ss.at[k], s_rs.at[k])
-        rows = []
-        for t in targets:
-            b = (z + t + N) % N
-            second = wide(b, k)
-            value = lat[k, b % 2, b // 2].astype(F32)
-            rows.append(
-                jnp.concatenate(
-                    [jnp.where(second, 0.0, value).astype(BF16), jnp.where(second, value, 0.0).astype(BF16)], axis=1
-                )
-            )
-        dec[k] = jnp.dot(
-            jnp.concatenate(rows, 0), d_buf[...].reshape(N * BLK, FEAT), preferred_element_type=F32
-        ).reshape(N, SUB, FEAT)
-        hop(k % 2, 0, k, dec[k, 0])
-
-    def z_step(k, step):
-        for direction in (k % 2, 1 - k % 2):
-            value = dec[k, 2 * step - 1 + direction]
-            if step > 1 or z_far(direction, k) == 4:
-                value = value + landed(direction, step - 1, k)
-            hop(direction, step, k, value)
-
-    def finish(k):
-        span = slice(k * SUB, (k + 1) * SUB)
-        total = dec[k, 7] + (landed(k % 2, 3, k) + landed(1 - k % 2, 3, k))
-        total += jnp.where(wide(z, k), meta[1, 0:1, :], meta[0, 0:1, :])
+    def landed(direction, step, h):
+        arrive(acc_in.at[direction, step, h], o_ss.at[direction, step, h], o_rs.at[direction, step, h])
+        return acc_in[direction, step, h].astype(F32)
+
+    def far(direction, h):
+        return h // (ZCH // 2) == direction
+
+    def z_start():
+        for i in range(ZCH // 2):
+            for direction in range(2):
+                h = direction * (ZCH // 2) + i
+                hop(direction, 0, h, dec[0, h * CHUNK:(h + 1) * CHUNK])
+
+    def z_step(step):
+        for i in range(ZCH):
+            for direction in range(2):
+                h = (i + (1 - direction) * (ZCH // 2)) % ZCH
+                value = dec[2 * step - 1 + direction, h * CHUNK:(h + 1) * CHUNK]
+                if step > 1 or far(direction, h):
+                    value = value + landed(direction, step - 1, h)
+                hop(direction, step, h, value)
+
+    def finish(h):
+        span = slice(h * CHUNK, (h + 1) * CHUNK)
+        total = dec[7, span] + (landed(0, 3, h) + landed(1, 3, h))
+        total += jnp.where(wide(mask[z, span, :]), meta[1, 0:1, :], meta[0, 0:1, :])
         rebuilt = total.astype(BF16)
         out[span, :] = rebuilt
         diff = rebuilt.astype(F32) - a_buf[z, span, :].astype(F32)
         sq = diff * diff
         square[span, :] = sq[:, 0:128] + sq[:, 128:256] + sq[:, 256:384] + sq[:, 384:512]
 
+    def settle(count):
+        for cp in pending[:count]:
+            cp.wait_send()
+        del pending[:count]
+
+    gathered = len(pending)
     encode(0)
     encode(1)
     pair_sum(0)
+    pair_sum(1)
+    d_arrive(1, 0)
+    d_send(2, 0)
     encode(2)
-    pair_sum(1)
     encode(3)
+    d_arrive(1, 1)
+    d_send(2, 1)
+    activate(0)
     pair_sum(2)
+    settle(gathered // 2)
+    activate(1)
     pair_sum(3)
-    gather_step((d_ring,), 1)
-    activate(0)
-    gather_step((d_ring,), 2)
-    activate(1)
+    d_arrive(2, 0)
+    d_arrive(2, 1)
+    d_send(3, 0)
+    d_send(3, 1)
+    share(0)
+    settle(gathered - gathered // 2)
     activate(2)
-    gather_step((d_ring,), 3)
+    d_arrive(3, 0)
+    d_arrive(3, 1)
+    decode(0)
+    z_start()
+    share(1)
     activate(3)
-    share(0)
-    gather_step((d_ring,), 4)
-    share(1)
-    decode(0)
+    decode(1)
+    z_step(1)
     share(2)
-    decode(1)
-    z_step(0, 1)
+    decode(2)
+    z_step(2)
     share(3)
-    decode(2)
-    z_step(1, 1)
     decode(3)
-    z_step(0, 2)
-    z_step(2, 1)
-    z_step(1, 2)
-    z_step(3, 1)
-    z_step(0, 3)
-    z_step(2, 2)
-    z_step(1, 3)
-    z_step(3, 2)
-    finish(0)
-    z_step(2, 3)
-    finish(1)
-    z_step(3, 3)
-    finish(2)
-    finish(3)
+    settle(len(pending) - 6 * ZCH)
+    z_step(3)
+    settle(len(pending) - 2 * ZCH)
+    for h in (0, 2, 1, 3):
+        finish(h)
 
     mine = jnp.sum(square[...].T, axis=0, keepdims=True)
     err_all[0] = jnp.broadcast_to(mine, (8, ROWS))
@@ -304,8 +366,7 @@
         arrive(err_all.at[k], e_ss.at[k], e_rs.at[k])
         total += err_all[k, 0:1, :]
     err[...] = total * (1.0 / D)
-    for cp in pending:
-        cp.wait_send()
+    settle(len(pending))
 
 
 def local(activations, expert_ids, pre_bias, enc_weight, enc_bias, dec_weight):
@@ -331,29 +392,29 @@
             pltpu.VMEM((2, 8, FEAT), F32),
             pltpu.VMEM((N, 8, ROWS), jnp.int32),
             pltpu.VMEM((N, ROWS, ROWS), F32),
-            pltpu.VMEM((K, NX * SUB, LATS), F32),
-            pltpu.VMEM((K, NX * SUB, LATS), BF16),
-            pltpu.VMEM((K, NX * SUB, LATS), BF16),
-            pltpu.VMEM((K, SUB, LATS), F32),
-            pltpu.VMEM((K, 3, SUB, LATS), BF16),
-            pltpu.VMEM((K, 3, SUB, LATS), BF16),
-            pltpu.VMEM((K, 2, NX, SUB, LATS), BF16),
-            pltpu.VMEM((K, N, SUB, FEAT), F32),
-            pltpu.VMEM((2, 4, K, SUB, FEAT), BF16),
-            pltpu.VMEM((2, 4, K, SUB, FEAT), BF16),
+            pltpu.VMEM((K, NX * MOST, LATS), F32),
+            pltpu.VMEM((K, NX * MOST, LATS), BF16),
+            pltpu.VMEM((K, NX * MOST, LATS), BF16),
+            pltpu.VMEM((K, MOST, LATS), F32),
+            pltpu.VMEM((K, 3, MOST, LATS), BF16),
+            pltpu.VMEM((K, 3, MOST, LATS), BF16),
+            pltpu.VMEM((K, 2, NX * MOST, LATS), BF16),
+            pltpu.VMEM((N, ROWS, FEAT), F32),
+            pltpu.VMEM((2, 4, ZCH, CHUNK, FEAT), BF16),
+            pltpu.VMEM((2, 4, ZCH, CHUNK, FEAT), BF16),
             pltpu.VMEM((ROWS, 128), F32),
             pltpu.VMEM((N, 8, ROWS), F32),
             dma((6,)),
             dma((2, 4, GATHER)), dma((2, 4, GATHER)),
             dma((2, 4, GATHER)), dma((2, 4, GATHER)),
-            dma((2, 4, DCH)), dma((2, 4, DCH)),
+            dma((2, 4, 4)), dma((2, 4, 4)),
             dma, dma,
             dma((N,)), dma((N,)),
             dma((K,)), dma((K,)),
             dma((K, 3)), dma((K, 3)),
             dma((K, 3)), dma((K, 3)),
             dma((K,)), dma((K,)),
-            dma((2, 4, K)), dma((2, 4, K)),
+            dma((2, 4, ZCH)), dma((2, 4, ZCH)),
             dma((N,)), dma((N,)),
         ],
         compiler_params=pltpu.CompilerParams(

time: 77.3 us -> 67.9 us (0.88)
  Pallas kernels: 74.4 us -> 65 us
    pallas_call x1, Pallas kernels: 74.4 us -> 65 us  [local(): pl.pallas_call(kernel, out_shape=(jax.ShapeDtypeStruct((ROWS, FEAT), BF16...]
where the time goes in v3:
time: 67.9 us; the launch traced here: 67.8 us
  Pallas kernels  65 us (96%)
  local copies, waits for them, and re-layouts  2.08 us (3%)
    pallas_call x1, Pallas kernels, local(): pl.pallas_call(kernel, out_shape=(jax.ShapeDtypeStruct((ROWS, FEAT), BF16...  65 us
    unnamed x4, local copies, waits for them, and re-layouts  2.08 us

profile of v3, /device:TPU:1, one launch (start us, length us, event | category | flops | bytes accessed | tf_op | source)
XLA Modules:
  0.0 67.8 jit_solution(2507792870362641907)
XLA Ops:
  0.6 65.0 %shard_map.77 = (bf16[128,512]{1,0:T(8,128)(2,1)}, f32[1,128]{1,0:T(1,128)}) custom-call(bf16[128,512]{1,0:T(8,128)(2,1)} %act.1, s32[1,128]{1,0:T(1,128)} %bitcast.2, f32[1,512]{1,0:T(1,128)} %pre_bias.1, bf16[1,512,128]{2,1,0:T(8,128)(2,1)} %enc_w.1, f32[1,4096]{1,0:T(1,128)} %enc_b.1, bf16[1,512,128]{2,1,0:T(8,128)(2,1)} %dec_w.1), custom_call_target="tpu_custom_call" | custom-call | tf_op jit(solution)/shard_map/pallas_call | solution.py:375
  65.7 0.0 copy-start
  65.7 1.6 %copy.10 = bf16[128,512]{1,0:T(8,128)(2,1)} copy(bf16[128,512]{1,0:T(8,128)(2,1)} %get-tuple-element.8) | data formatting | bytes 262144
  67.3 0.0 copy-done
  67.3 0.5 copy.11
Async XLA Ops:
  65.7 1.6 %copy-start = (f32[1,128]{1,0:T(1,128)S(1)}, f32[1,128]{1,0:T(1,128)}, u32[]{:S(2)}) copy-start(f32[1,128]{1,0:T(1,128)} %get-tuple-element.5) | copy-start | bytes 1540

commit v4 on v3

--- a/solution.py
+++ b/solution.py
@@ -97,6 +97,60 @@
     ]
     for cp in loads:
         cp.start()
+    pl.semaphore_wait(barrier, len(greet))
+
+    def ring_piece(buf, slot_of, coord, chunks, direction, step, chunk):
+        sign = 1 if direction == 0 else -1
+        block = slot_of((coord - step * sign + N) % N)
+        size = buf.shape[1] // chunks
+        return buf.at[block, pl.ds(chunk * size, size)]
+
+    def ring_send(buf, first, slot_of, coord, chunks, to, ss, rs, direction, step, chunk):
+        ref = ring_piece(buf, slot_of, coord, chunks, direction, step, chunk)
+        size = buf.shape[1] // chunks
+        src = first.at[pl.ds(chunk * size, size)] if step == 0 else ref
+        sign = 1 if direction == 0 else -1
+        send(src, ref, ss.at[direction, step, chunk], rs.at[direction, step, chunk], to(sign))
+
+    def ring_arrive(buf, slot_of, coord, chunks, ss, rs, direction, step, chunk):
+        ref = ring_piece(buf, slot_of, coord, chunks, direction, step + 1, chunk)
+        arrive(ref, ss.at[direction, step, chunk], rs.at[direction, step, chunk])
+
+    a_ring = (a_buf, act, lambda b: b, z, GATHER, z_at, a_ss, a_rs)
+    w_ring = (w_buf, enc_w.at[0], w_slot, y, GATHER, y_at, w_ss, w_rs)
+    def gather_step(rings, step):
+        for chunk in range(GATHER):
+            for buf, first, slot_of, coord, chunks, to, ss, rs in rings:
+                for direction in range(2):
+                    steps = ring_steps(direction, chunk, chunks)
+                    if 1 <= step <= steps:
+                        ring_arrive(buf, slot_of, coord, chunks, ss, rs, direction, step - 1, chunk)
+                    if step < steps:
+                        ring_send(buf, first, slot_of, coord, chunks, to, ss, rs, direction, step, chunk)
+
+    def spread(yy):
+        lanes = pl.ds(pl.multiple_of((yy // 2) * BLK, BLK), BLK)
+        w_cat[yy % 2, :, lanes] = w_buf[w_slot(yy)]
+
+    def d_piece(direction, hop, i):
+        piece = (i + 2 * direction) % 4
+        block = w_slot((y - hop * (1 - 2 * direction) + N) % N)
+        return d_buf.at[block, pl.ds(piece * (BLK // 4), BLK // 4)]
+
+    def d_send(hop, i):
+        for direction in range(2):
+            ref = d_piece(direction, hop, i)
+            send(ref, ref, d_ss.at[direction, hop, i], d_rs.at[direction, hop, i], y_at(1 - 2 * direction))
+
+    def d_arrive(hop, i):
+        for direction in range(2):
+            arrive(d_piece(direction, hop + 1, i), d_ss.at[direction, hop, i], d_rs.at[direction, hop, i])
+
+    def d_pass(hop, i):
+        d_arrive(hop - 1, i)
+        d_send(hop, i)
+
+    gather_step((w_ring, a_ring), 0)
     for cp in loads:
         cp.wait()
     d_buf[w_slot(y)] = d_raw[...].astype(F32).T.astype(BF16)
@@ -104,60 +158,6 @@
     for q in range(4):
         meta[dp, 1:2, q * BLK:(q + 1) * BLK] = eb_raw[0:1, pl.ds(pl.multiple_of((q * 8 + z) * BLK, BLK), BLK)]
     ids_all[z] = jnp.broadcast_to(ids_raw[...], (8, ROWS))
-
-    pl.semaphore_wait(barrier, len(greet))
-
-    def ring_piece(buf, slot_of, coord, chunks, direction, step, chunk):
-        sign = 1 if direction == 0 else -1
-        block = slot_of((coord - step * sign + N) % N)
-        size = buf.shape[1] // chunks
-        return buf.at[block, pl.ds(chunk * size, size)]
-
-    def ring_send(buf, slot_of, coord, chunks, to, ss, rs, direction, step, chunk):
-        ref = ring_piece(buf, slot_of, coord, chunks, direction, step, chunk)
-        sign = 1 if direction == 0 else -1
-        send(ref, ref, ss.at[direction, step, chunk], rs.at[direction, step, chunk], to(sign))
-
-    def ring_arrive(buf, slot_of, coord, chunks, ss, rs, direction, step, chunk):
-        ref = ring_piece(buf, slot_of, coord, chunks, direction, step + 1, chunk)
-        arrive(ref, ss.at[direction, step, chunk], rs.at[direction, step, chunk])
-
-    a_ring = (a_buf, lambda b: b, z, GATHER, z_at, a_ss, a_rs)
-    w_ring = (w_buf, w_slot, y, GATHER, y_at, w_ss, w_rs)
-    def gather_step(rings, step):
-        for chunk in range(GATHER):
-            for buf, slot_of, coord, chunks, to, ss, rs in rings:
-                for direction in range(2):
-                    steps = ring_steps(direction, chunk, chunks)
-                    if 1 <= step <= steps:
-                        ring_arrive(buf, slot_of, coord, chunks, ss, rs, direction, step - 1, chunk)
-                    if step < steps:
-                        ring_send(buf, slot_of, coord, chunks, to, ss, rs, direction, step, chunk)
-
-    def spread(yy):
-        lanes = pl.ds(pl.multiple_of((yy // 2) * BLK, BLK), BLK)
-        w_cat[yy % 2, :, lanes] = w_buf[w_slot(yy)]
-
-    def d_piece(direction, hop, piece):
-        size = BLK // 4 if hop == 0 else BLK // 2
-        block = w_slot((y - hop * (1 - 2 * direction) + N) % N)
-        return d_buf.at[block, pl.ds(piece * size, size)], d_ss.at[direction, hop, piece], d_rs.at[direction, hop, piece]
-
-    def d_send(hop, piece):
-        for direction in range(2):
-            if hop < 3 or piece == direction:
-                ref, ss, rs = d_piece(direction, hop, piece)
-                send(ref, ref, ss, rs, y_at(1 - 2 * direction))
-
-    def d_arrive(hop, piece):
-        for direction in range(2):
-            if hop < 3 or piece == direction:
-                ref, ss, rs = d_piece(direction, hop, piece)
-                size = ref.shape[0]
-                block = w_slot((y - (hop + 1) * (1 - 2 * direction) + N) % N)
-                arrive(d_buf.at[block, pl.ds(piece * size, size)], ss, rs)
-
-    gather_step((a_ring, w_ring), 0)
     send(meta.at[dp], meta.at[dp], m_ss, m_rs, at(y + 1 - 2 * dp, z, feature))
     for k in range(1, N):
         send(ids_all.at[z], ids_all.at[z], i_ss.at[k], i_rs.at[k], z_at(k))
@@ -168,28 +168,26 @@
 
     mask_of(z)
     spread(y)
-    gather_step((a_ring, w_ring), 1)
+    gather_step((w_ring, a_ring), 1)
     d_send(0, 1)
     for k in range(1, N):
         src = (z - k + N) % N
         arrive(ids_all.at[src], i_ss.at[k], i_rs.at[k])
         mask_of(src)
     arrive(meta.at[1 - dp], m_ss, m_rs)
-    gather_step((a_ring, w_ring), 2)
+    gather_step((w_ring, a_ring), 2)
     d_send(0, 2)
     d_send(0, 3)
     spread((y + 1) % N)
     spread((y + 7) % N)
-    gather_step((a_ring, w_ring), 3)
+    gather_step((w_ring, a_ring), 3)
     spread((y + 2) % N)
     spread((y + 6) % N)
-    for piece in range(4):
-        d_arrive(0, piece)
-    d_send(1, 0)
-    d_send(1, 1)
+    for i in range(4):
+        d_pass(1, i)
     spread((y + 3) % N)
     spread((y + 5) % N)
-    gather_step((a_ring, w_ring), 4)
+    gather_step((w_ring, a_ring), 4)
     spread((y + 4) % N)
 
     def wide(tile):
@@ -319,32 +317,32 @@
     encode(0)
     encode(1)
     pair_sum(0)
+    d_pass(2, 0)
+    encode(2)
     pair_sum(1)
-    d_arrive(1, 0)
-    d_send(2, 0)
-    encode(2)
+    d_pass(2, 1)
     encode(3)
-    d_arrive(1, 1)
-    d_send(2, 1)
+    pair_sum(2)
+    d_pass(2, 2)
+    d_pass(2, 3)
+    settle(gathered // 2)
     activate(0)
-    pair_sum(2)
-    settle(gathered // 2)
+    d_pass(3, 0)
     activate(1)
+    d_pass(3, 1)
     pair_sum(3)
-    d_arrive(2, 0)
-    d_arrive(2, 1)
-    d_send(3, 0)
-    d_send(3, 1)
+    activate(2)
     share(0)
     settle(gathered - gathered // 2)
-    activate(2)
+    d_arrive(2, 2)
+    d_arrive(2, 3)
     d_arrive(3, 0)
     d_arrive(3, 1)
     decode(0)
     z_start()
     share(1)
+    decode(1)
     activate(3)
-    decode(1)
     z_step(1)
     share(2)
     decode(2)

time: 67.9 us -> 66.7 us (0.982)
  Pallas kernels: 65 us -> 63.8 us
    pallas_call x1, Pallas kernels: 65 us -> 63.8 us  [local(): pl.pallas_call(kernel, out_shape=(jax.ShapeDtypeStruct((ROWS, FEAT), BF16...]
where the time goes in v4:
time: 66.7 us; the launch traced here: 66.5 us
  Pallas kernels  63.8 us (96%)
  local copies, waits for them, and re-layouts  2.08 us (3%)
    pallas_call x1, Pallas kernels, local(): pl.pallas_call(kernel, out_shape=(jax.ShapeDtypeStruct((ROWS, FEAT), BF16...  63.8 us
    unnamed x4, local copies, waits for them, and re-layouts  2.08 us

profile of v4, /device:TPU:1, one launch (start us, length us, event | category | flops | bytes accessed | tf_op | source)
XLA Modules:
  0.0 66.5 jit_solution(5427677667822212948)
XLA Ops:
  0.6 63.8 %shard_map.77 = (bf16[128,512]{1,0:T(8,128)(2,1)}, f32[1,128]{1,0:T(1,128)}) custom-call(bf16[128,512]{1,0:T(8,128)(2,1)} %act.1, s32[1,128]{1,0:T(1,128)} %bitcast.2, f32[1,512]{1,0:T(1,128)} %pre_bias.1, bf16[1,512,128]{2,1,0:T(8,128)(2,1)} %enc_w.1, f32[1,4096]{1,0:T(1,128)} %enc_b.1, bf16[1,512,128]{2,1,0:T(8,128)(2,1)} %dec_w.1), custom_call_target="tpu_custom_call" | custom-call | tf_op jit(solution)/shard_map/pallas_call | solution.py:373
  64.4 0.0 copy-start
  64.4 1.6 %copy.10 = bf16[128,512]{1,0:T(8,128)(2,1)} copy(bf16[128,512]{1,0:T(8,128)(2,1)} %get-tuple-element.8) | data formatting | bytes 262144
  66.0 0.0 copy-done
  66.0 0.5 copy.11
Async XLA Ops:
  64.4 1.6 %copy-start = (f32[1,128]{1,0:T(1,128)S(1)}, f32[1,128]{1,0:T(1,128)}, u32[]{:S(2)}) copy-start(f32[1,128]{1,0:T(1,128)} %get-tuple-element.5) | copy-start | bytes 1540

commit v5 on v4

--- a/solution.py
+++ b/solution.py
@@ -77,7 +77,7 @@
         ).wait_recv()
 
     barrier = pltpu.get_barrier_semaphore()
-    greet = [z_at(k) for k in range(1, N)] + [y_at(1), y_at(-1)]
+    greet = [y_at(1), y_at(-1), z_at(1), z_at(-1)] + [z_at(k) for k in range(2, N - 1)]
     greet += [at(y, z, (feature + k) % 8) for k in range(1, 8)]
     for dev in greet:
         pl.semaphore_signal(barrier, inc=1, device_id=dev, device_id_type=MESH)
@@ -95,8 +95,6 @@
             )
         )
     ]
-    for cp in loads:
-        cp.start()
     pl.semaphore_wait(barrier, len(greet))
 
     def ring_piece(buf, slot_of, coord, chunks, direction, step, chunk):
@@ -152,6 +150,8 @@
 
     gather_step((w_ring, a_ring), 0)
     for cp in loads:
+        cp.start()
+    for cp in loads:
         cp.wait()
     d_buf[w_slot(y)] = d_raw[...].astype(F32).T.astype(BF16)
     meta[dp, 0:1, :] = pb_raw[...]
@@ -166,18 +166,19 @@
     def mask_of(b):
         mask[b] = jnp.broadcast_to(ids_all[b, 0:1, :].astype(F32), (ROWS, ROWS)).T
 
-    mask_of(z)
     spread(y)
     gather_step((w_ring, a_ring), 1)
     d_send(0, 1)
     for k in range(1, N):
-        src = (z - k + N) % N
-        arrive(ids_all.at[src], i_ss.at[k], i_rs.at[k])
-        mask_of(src)
+        arrive(ids_all.at[(z - k + N) % N], i_ss.at[k], i_rs.at[k])
     arrive(meta.at[1 - dp], m_ss, m_rs)
+    mask_of(z)
+    mask_of((z + 4) % N)
     gather_step((w_ring, a_ring), 2)
     d_send(0, 2)
     d_send(0, 3)
+    for k in (1, 2, 3):
+        mask_of((z + k) % N)
     spread((y + 1) % N)
     spread((y + 7) % N)
     gather_step((w_ring, a_ring), 3)
@@ -185,6 +186,8 @@
     spread((y + 6) % N)
     for i in range(4):
         d_pass(1, i)
+    for k in (5, 6, 7):
+        mask_of((z + k) % N)
     spread((y + 3) % N)
     spread((y + 5) % N)
     gather_step((w_ring, a_ring), 4)
@@ -342,8 +345,8 @@
     z_start()
     share(1)
     decode(1)
+    z_step(1)
     activate(3)
-    z_step(1)
     share(2)
     decode(2)
     z_step(2)

time: 66.7 us -> 65.9 us (0.988)
  Pallas kernels: 63.8 us -> 62.9 us
    pallas_call x1, Pallas kernels: 63.8 us -> 62.9 us  [local(): pl.pallas_call(kernel, out_shape=(jax.ShapeDtypeStruct((ROWS, FEAT), BF16...]
where the time goes in v5:
time: 65.9 us; the launch traced here: 65.7 us
  Pallas kernels  62.9 us (95%)
  local copies, waits for them, and re-layouts  2.08 us (3%)
    pallas_call x1, Pallas kernels, local(): pl.pallas_call(kernel, out_shape=(jax.ShapeDtypeStruct((ROWS, FEAT), BF16...  62.9 us
    unnamed x4, local copies, waits for them, and re-layouts  2.08 us

profile of v5, /device:TPU:1, one launch (start us, length us, event | category | flops | bytes accessed | tf_op | source)
XLA Modules:
  0.0 65.7 jit_solution(25122521565533247)
XLA Ops:
  0.6 62.9 %shard_map.77 = (bf16[128,512]{1,0:T(8,128)(2,1)}, f32[1,128]{1,0:T(1,128)}) custom-call(bf16[128,512]{1,0:T(8,128)(2,1)} %act.1, s32[1,128]{1,0:T(1,128)} %bitcast.2, f32[1,512]{1,0:T(1,128)} %pre_bias.1, bf16[1,512,128]{2,1,0:T(8,128)(2,1)} %enc_w.1, f32[1,4096]{1,0:T(1,128)} %enc_b.1, bf16[1,512,128]{2,1,0:T(8,128)(2,1)} %dec_w.1), custom_call_target="tpu_custom_call" | custom-call | tf_op jit(solution)/shard_map/pallas_call | solution.py:376
  63.6 0.0 copy-start
  63.6 1.6 %copy.10 = bf16[128,512]{1,0:T(8,128)(2,1)} copy(bf16[128,512]{1,0:T(8,128)(2,1)} %get-tuple-element.8) | data formatting | bytes 262144
  65.2 0.0 copy-done
  65.2 0.5 copy.11
Async XLA Ops:
  63.6 1.6 %copy-start = (f32[1,128]{1,0:T(1,128)S(1)}, f32[1,128]{1,0:T(1,128)}, u32[]{:S(2)}) copy-start(f32[1,128]{1,0:T(1,128)} %get-tuple-element.5) | copy-start | bytes 1540

commit v6 on v5

--- a/solution.py
+++ b/solution.py
@@ -333,9 +333,9 @@
     d_pass(3, 0)
     activate(1)
     d_pass(3, 1)
+    share(0)
+    activate(2)
     pair_sum(3)
-    activate(2)
-    share(0)
     settle(gathered - gathered // 2)
     d_arrive(2, 2)
     d_arrive(2, 3)
@@ -352,19 +352,18 @@
     z_step(2)
     share(3)
     decode(3)
-    settle(len(pending) - 6 * ZCH)
     z_step(3)
     settle(len(pending) - 2 * ZCH)
-    for h in (0, 2, 1, 3):
+    for h in (2, 0, 3, 1):
         finish(h)
 
     mine = jnp.sum(square[...].T, axis=0, keepdims=True)
     err_all[0] = jnp.broadcast_to(mine, (8, ROWS))
     for k in range(1, 8):
-        send(err_all.at[0], err_all.at[k], e_ss.at[k], e_rs.at[k], at(y, z, (feature + k) % 8))
+        send(err_all.at[0, pl.ds(0, 1)], err_all.at[k, pl.ds(0, 1)], e_ss.at[k], e_rs.at[k], at(y, z, (feature + k) % 8))
     total = mine
     for k in range(1, 8):
-        arrive(err_all.at[k], e_ss.at[k], e_rs.at[k])
+        arrive(err_all.at[k, pl.ds(0, 1)], e_ss.at[k], e_rs.at[k])
         total += err_all[k, 0:1, :]
     err[...] = total * (1.0 / D)
     settle(len(pending))

time: 65.9 us -> 65.5 us (level)
  no operation moved by 1% of the time
where the time goes in v6:
time: 65.5 us; the launch traced here: 65.3 us
  Pallas kernels  62.6 us (96%)
  local copies, waits for them, and re-layouts  2.08 us (3%)
    pallas_call x1, Pallas kernels, local(): pl.pallas_call(kernel, out_shape=(jax.ShapeDtypeStruct((ROWS, FEAT), BF16...  62.6 us
    unnamed x4, local copies, waits for them, and re-layouts  2.08 us

profile of v6, /device:TPU:1, one launch (start us, length us, event | category | flops | bytes accessed | tf_op | source)
XLA Modules:
  0.0 65.3 jit_solution(14818086402349642289)
XLA Ops:
  0.6 62.6 %shard_map.77 = (bf16[128,512]{1,0:T(8,128)(2,1)}, f32[1,128]{1,0:T(1,128)}) custom-call(bf16[128,512]{1,0:T(8,128)(2,1)} %act.1, s32[1,128]{1,0:T(1,128)} %bitcast.2, f32[1,512]{1,0:T(1,128)} %pre_bias.1, bf16[1,512,128]{2,1,0:T(8,128)(2,1)} %enc_w.1, f32[1,4096]{1,0:T(1,128)} %enc_b.1, bf16[1,512,128]{2,1,0:T(8,128)(2,1)} %dec_w.1), custom_call_target="tpu_custom_call" | custom-call | tf_op jit(solution)/shard_map/pallas_call | solution.py:375
  63.2 0.0 copy-start
  63.2 1.6 %copy.10 = bf16[128,512]{1,0:T(8,128)(2,1)} copy(bf16[128,512]{1,0:T(8,128)(2,1)} %get-tuple-element.8) | data formatting | bytes 262144
  64.8 0.0 copy-done
  64.8 0.5 copy.11
Async XLA Ops:
  63.2 1.6 %copy-start = (f32[1,128]{1,0:T(1,128)S(1)}, f32[1,128]{1,0:T(1,128)}, u32[]{:S(2)}) copy-start(f32[1,128]{1,0:T(1,128)} %get-tuple-element.5) | copy-start | bytes 1540
